TPU v7x, 256 devices: a whole 4x4x8 slice. The times are simulated.
256 devices in a mesh: chan: 128 (over y, z, x_lo, core), tm: 2 (over x_hi).
Axes of the slice: x: 4 (x_hi: 2, x_lo: 2; x = x_hi * 2 + x_lo), y: 4, z: 8, core: 2. Of those that a mesh axis runs over, the one named last changes fastest.
Arguments:
- traces: float32 [4, 1024, 768], P('tm', 'chan'), may hold values from -6 to 6
- lengths: int32 [4], replicated, may hold values from 1 to 768, 2304 in all
- mask: int32 [1024], P('chan'), may hold values 0 or 1
Outputs:
- correlations: float32 [1024, 1024, 256], P(('chan', 'tm'))
Inputs may be any that keep to these rules, and one draw needn't show every extreme that they name: `lengths`: live samples of each sub-window; together they hold 2304 samples and the longest holds exactly 768.
All inputs are finite; a program needn't handle non-finite values. No bound on the sum of `mask` on one device may be relied on, other than what follows from the above.
Results may differ from a plain program's by a relative error of at most 0.0043.
Values may be sent and summed in bfloat16 or wider, within the bound.
No kernel may reach another device: no remote copies, remote signals or barrier semaphores. Data moves between devices by JAX's collectives and lax.ppermute only.
A program may use at most 128 MiB of HBM per device.

v0:
```python
import math
import jax
import jax.numpy as jnp
from jax import lax
from jax.sharding import PartitionSpec as P

NFFT = 1024
LAG = 128
F = 512


def dft_table(seg_len, nfft, nfreq):
    sample_idx = jnp.arange(seg_len, dtype=jnp.int32)
    freq_idx = jnp.arange(nfreq, dtype=jnp.int32)
    product = jnp.mod(sample_idx[:, None] * freq_idx[None, :], nfft).astype(jnp.float32)
    theta = product * (2.0 * math.pi / nfft)
    return jnp.concatenate([jnp.cos(theta), -jnp.sin(theta)], axis=1)


def lag_table(nfft, nfreq, max_lag, sub_total):
    freq_idx = jnp.arange(nfreq, dtype=jnp.int32)
    lag_idx = jnp.arange(2 * max_lag, dtype=jnp.int32) - max_lag
    product = jnp.mod(freq_idx[:, None] * lag_idx[None, :], nfft).astype(jnp.float32)
    phase = product * (2.0 * math.pi / nfft)
    weight = jnp.where(freq_idx == 0, 1.0, 2.0).astype(jnp.float32)[:, None] / math.sqrt(
        nfreq * sub_total
    )
    return jnp.concatenate([weight * jnp.cos(phase), -weight * jnp.sin(phase)], axis=0).astype(
        jnp.bfloat16
    )


def whiten_spectra(traces, lengths, mask):
    seg_len = traces.shape[2]
    live = (jnp.arange(seg_len, dtype=jnp.int32)[None, :] < lengths[:, None]).astype(jnp.float32)
    counted = lengths.astype(jnp.float32)
    average = jnp.sum(traces * live[:, None, :], axis=-1) / counted[:, None]
    centred = (traces - average[:, :, None]) * live[:, None, :]
    table = dft_table(seg_len, NFFT, F)
    spectrum = jnp.dot(
        centred.reshape(-1, seg_len),
        table,
        precision=lax.Precision.HIGHEST,
        preferred_element_type=jnp.float32,
    )
    spectrum = spectrum.reshape(traces.shape[0], traces.shape[1], 2 * F)
    power = spectrum[..., :F] ** 2 + spectrum[..., F:] ** 2
    level = jnp.mean(power, axis=-1, keepdims=True)
    factor = 1.0 / jnp.sqrt(power + 0.01 * level + 1e-06)
    factor = jnp.concatenate([factor, factor], axis=-1)
    return (spectrum * factor * mask.astype(jnp.float32)[None, :, None]).astype(jnp.bfloat16)


def cross_spectrum(own_spec, other_spec):
    nfreq = own_spec.shape[-1] // 2
    own_re = own_spec[..., :nfreq]
    own_im = own_spec[..., nfreq:]
    other_re = other_spec[..., :nfreq]
    other_im = other_spec[..., nfreq:]
    real_part = jnp.einsum(
        "kif,kjf->ijf", own_re, other_re, preferred_element_type=jnp.float32
    ) + jnp.einsum("kif,kjf->ijf", own_im, other_im, preferred_element_type=jnp.float32)
    imag_part = jnp.einsum(
        "kif,kjf->ijf", own_im, other_re, preferred_element_type=jnp.float32
    ) - jnp.einsum("kif,kjf->ijf", own_re, other_im, preferred_element_type=jnp.float32)
    return jnp.concatenate([real_part, imag_part], axis=-1).astype(jnp.bfloat16)


def place_lags(running, own_spec, incoming, begin_col, lag_matrix):
    column_count = incoming.shape[1]
    slab_cols = 128

    def one_slab(slab, offset, current):
        half_spectra = cross_spectrum(own_spec, slab)
        lag_values = jnp.dot(
            half_spectra.reshape(-1, half_spectra.shape[-1]),
            lag_matrix,
            preferred_element_type=jnp.float32,
        )
        lag_values = lag_values.reshape(own_spec.shape[1], slab.shape[1], lag_matrix.shape[1])
        return lax.dynamic_update_slice(
            current, lag_values, (jnp.int32(0), jnp.asarray(offset, jnp.int32), jnp.int32(0))
        )

    def loop_body(slab_index, current):
        slab = lax.dynamic_slice_in_dim(incoming, slab_index * slab_cols, slab_cols, 1)
        return one_slab(slab, begin_col + slab_index * slab_cols, current)

    return lax.fori_loop(0, column_count // slab_cols, loop_body, running)


def local(traces, lengths, mask):
    sub_count = traces.shape[0]
    own_rows = traces.shape[1]
    time_groups = lax.axis_size("tm")
    local_lengths = lax.dynamic_slice_in_dim(lengths, lax.axis_index("tm") * sub_count, sub_count)
    spectra = whiten_spectra(traces, local_lengths, mask)
    lag_matrix = lag_table(NFFT, F, LAG, sub_count * time_groups)
    channel_total = own_rows * lax.axis_size("chan")
    empty_lags = jnp.zeros((own_rows, channel_total, 2 * LAG), jnp.float32)
    partial_lags = place_lags(
        empty_lags,
        spectra,
        lax.all_gather(spectra, "chan", axis=1, tiled=True),
        jnp.int32(0),
        lag_matrix,
    )
    return lax.psum_scatter(partial_lags, "tm", scatter_dimension=0, tiled=True)


def solution(mesh):
    placed = (P("tm", "chan", None), P(), P("chan"))
    return jax.shard_map(
        local, mesh=mesh, in_specs=placed, out_specs=P(("chan", "tm"), None, None), check_vma=False
    )
```

profile of v0, /device:TPU:1, one launch (start us, length us, event | category | flops | bytes accessed | tf_op | source)
XLA Modules:
  0.0 562.4 jit_solution(10639168242448990964)
XLA Ops:
  6.5 6.2 %sine_negate_fusion = (f32[768,512]{1,0:T(8,128)S(1)}, f32[768,512]{1,0:T(8,128)S(1)}) fusion(), kind=kLoop, calls=%fused_computation.23 | loop fusion | flops 5898240 | bytes 3145728 | tf_op jit(solution)/shard_map/neg | solution.py:17
  19.0 216.1 %all-gather.2.cloned.1.call-done = bf16[2,1024,1024]{2,1,0:T(8,128)(2,1)} async-done(((bf16[2,8,1024]{2,1,0:T(8,128)(2,1)}), bf16[2,1024,1024]{2,1,0:T(8,128)(2,1)}) %all-gather.2.cloned.1.call-update) | async-done | bytes 4194320 | tf_op jit(solution)/shard_map/all_gather | solution.py:104
  235.1 3.9 broadcast_in_dim.8
  239.0 211.6 %while.13 = (s32[]{:T(128)}, f32[8,1024,256]{2,1,0:T(8,128)}, bf16[2,1024,1024]{2,1,0:T(8,128)(2,1)}, bf16[2,8,1024]{2,1,0:T(8,128)(2,1)S(1)}, bf16[1024,256]{1,...) while((s32[]{:T(128)}, f32[8,1024,256]{2,1,0:T(8,128)}, ...), condition=%wide.region_3.4_spmd, body=%wide.region_2.3_spmd.sunk | while | flops 551550976 | bytes 44761288 | solution.py:89
  252.0 3.0 copy.26
  257.2 2.9 copy.25
  260.1 3.7 fusion.83
  278.5 3.0 copy.26
  283.6 2.9 copy.25
  286.5 3.7 fusion.83
  304.9 3.0 copy.26
  310.0 2.9 copy.25
  313.0 3.7 fusion.83
  331.4 3.0 copy.26
  339.4 3.7 fusion.83
  357.8 3.0 copy.26
  365.9 3.7 fusion.83
  384.3 3.0 copy.26
  392.3 3.7 fusion.83
  410.7 3.0 copy.26
  418.8 3.7 fusion.83
  437.2 3.0 copy.26
  445.2 3.7 fusion.83
  450.6 104.9 %reduce-scatter.2.cloned.1.call-done = f32[4,1024,256]{2,1,0:T(8,128)} async-done(((f32[8,1024,256]{2,1,0:T(8,128)}), f32[4,1024,256]{2,1,0:T(8,128)}) %reduce-scatter.2.cloned.1.call-update) | async-done | bytes 4194320 | tf_op jit(solution)/shard_map/reduce_scatter | solution.py:108
  (151 shorter events, 155.3 us)
Async XLA Ops:
  6.5 6.2 %copy-start.4 = (s32[8]{0:T(128)S(1)}, s32[8]{0:T(128)}, u32[]{:S(2)}) copy-start(s32[8]{0:T(128)} %param.7) | copy-start | bytes 100
  6.5 6.2 %copy-start.3 = (s32[4]{0:T(128)S(1)}, s32[4]{0:T(128)}, u32[]{:S(2)}) copy-start(s32[4]{0:T(128)} %param.6) | copy-start | bytes 52
  6.5 6.4 %copy-start.2 = (f32[2,8,768]{2,1,0:T(8,128)S(1)}, f32[2,8,768]{2,1,0:T(8,128)}, u32[]{:S(2)}) copy-start(f32[2,8,768]{2,1,0:T(8,128)} %param.5) | copy-start | bytes 147460
  6.5 228.5 %all-gather.2.cloned.1.call-start = ((), (), s32[]{:S(2)}) async-start(), calls=%async_computation.1 | async-start | bytes 4227072 | tf_op jit(solution)/shard_map/all_gather | solution.py:104
  15.6 539.9 %reduce-scatter.2.cloned.1.call-start = ((), (), s32[]{:S(2)}) async-start(), calls=%async_computation.2 | async-start | bytes 12582912 | tf_op jit(solution)/shard_map/reduce_scatter | solution.py:108
  19.0 220.0 %copy-start = (bf16[2,8,1024]{2,1,0:T(8,128)(2,1)S(1)}, bf16[2,8,1024]{2,1,0:T(8,128)(2,1)}, u32[]{:S(2)}) copy-start(bf16[2,8,1024]{2,1,0:T(8,128)(2,1)} %fusion.28) | copy-start | bytes 98308
  260.1 3.7 copy-start.1
  286.5 3.7 copy-start.1
  313.0 3.7 copy-start.1
  339.4 3.7 copy-start.1
  365.9 3.7 copy-start.1
  392.3 3.7 copy-start.1
  418.8 3.7 copy-start.1
  445.2 3.7 copy-start.1
Sparse Core Ops, SparseCore 0:
  15.7 219.3 all-gather.1
  450.8 104.7 reduce-scatter.1
where the time goes:
time: 563 us; the launch traced here: 562 us
  waiting for transfers between devices  321 us (57%)
  local copies, waits for them, and re-layouts  104 us (18%)
  matrix products  83.3 us (15%)
  other arithmetic  39.8 us (7%)
  between operations  13.5 us (2%)
    all_gather x1, waiting for transfers between devices, local(): lax.all_gather(spectra, 'chan', axis=1, tiled=True)  216 us
    reduce_scatter x1, waiting for transfers between devices, local(): return lax.psum_scatter(partial_lags, 'tm', scatter_dimension=0, tiled=True)  105 us
    add x8, other arithmetic, cross_spectrum(): jnp.einsum('kif,kjf->ijf', own_re, other_re, preferred_element_type=jnp.f...  29.3 us
    dot_general x8, local copies, waits for them, and re-layouts, cross_spectrum(): jnp.einsum('kif,kjf->ijf', own_im, other_re, preferred_element_type=jnp.f...  24 us
    dot_general x8, local copies, waits for them, and re-layouts, cross_spectrum(): jnp.einsum('kif,kjf->ijf', own_im, other_im, preferred_element_type=jnp.f...  23.5 us
    dot_general x8, local copies, waits for them, and re-layouts, cross_spectrum(): jnp.einsum('kif,kjf->ijf', own_re, other_re, preferred_element_type=jnp.f...  23.4 us
    dot_general x8, matrix products, cross_spectrum(): jnp.einsum('kif,kjf->ijf', own_re, other_im, preferred_element_type=jnp.f...  17 us
    dot_general x8, matrix products, cross_spectrum(): jnp.einsum('kif,kjf->ijf', own_re, other_re, preferred_element_type=jnp.f...  17 us
  transfers between devices with their start and end apart: 2, of which 2 were waited for; matrix products, arithmetic and copies ran while one was open for 1% of the time, Pallas kernels for 0%

commit v1 on v0

--- a/solution.py
+++ b/solution.py
@@ -7,6 +7,9 @@
 NFFT = 1024
 LAG = 128
 F = 512
+pass_the_bands = lambda point, d0: jnp.concatenate(
+    lax.all_to_all(jnp.stack(lax.axis_size("chan") * [point], 0), "chan", 0, 0), d0
+)
 
 
 def dft_table(seg_len, nfft, nfreq):
@@ -99,11 +102,7 @@
     channel_total = own_rows * lax.axis_size("chan")
     empty_lags = jnp.zeros((own_rows, channel_total, 2 * LAG), jnp.float32)
     partial_lags = place_lags(
-        empty_lags,
-        spectra,
-        lax.all_gather(spectra, "chan", axis=1, tiled=True),
-        jnp.int32(0),
-        lag_matrix,
+        empty_lags, spectra, pass_the_bands(spectra, 1), jnp.int32(0), lag_matrix
     )
     return lax.psum_scatter(partial_lags, "tm", scatter_dimension=0, tiled=True)
 

time: 563 us -> 346 us (0.61)
  waiting for transfers between devices: 321 us -> 194 us
  local copies, waits for them, and re-layouts: 104 us -> 58.9 us
  matrix products: 83.3 us -> 49.8 us
  other arithmetic: 39.8 us -> 11.4 us
  starting transfers between devices: 0.22 us -> 15.5 us
    all_gather x1 -> x0, waiting for transfers between devices: 216 us -> none  [local(): lax.all_gather(spectra, 'chan', axis=1, tiled=True)]
    all_to_all x0 -> x1, waiting for transfers between devices: none -> 90.2 us  [lax.all_to_all(jnp.stack(lax.axis_size('chan') * [point], 0), 'chan', 0, 0)]
    add x8 -> x0, other arithmetic: 29.3 us -> none  [cross_spectrum(): jnp.einsum('kif,kjf->ijf', own_re, other_re, preferred_element_type=jnp.f...]
    dot_general x8, local copies, waits for them, and re-layouts: 23.4 us -> 1.46 us  [cross_spectrum(): jnp.einsum('kif,kjf->ijf', own_re, other_re, preferred_element_type=jnp.f...]
    dot_general x8, local copies, waits for them, and re-layouts: 24 us -> 7.16 us  [cross_spectrum(): jnp.einsum('kif,kjf->ijf', own_im, other_re, preferred_element_type=jnp.f...]
    dot_general x8, local copies, waits for them, and re-layouts: 23.5 us -> 7.24 us  [cross_spectrum(): jnp.einsum('kif,kjf->ijf', own_im, other_im, preferred_element_type=jnp.f...]
    all_to_all x0 -> x1, starting transfers between devices: none -> 15.3 us  [lax.all_to_all(jnp.stack(lax.axis_size('chan') * [point], 0), 'chan', 0, 0)]
    slice x48 -> x0, local copies, waits for them, and re-layouts: 13.9 us -> none  [the longest x16 9.97 us: cross_spectrum(): other_im = other_spec[..., nfreq:]]
where the time goes in v1:
time: 346 us; the launch traced here: 344 us
  waiting for transfers between devices  194 us (56%)
  local copies, waits for them, and re-layouts  58.9 us (17%)
  matrix products  49.8 us (14%)
  starting transfers between devices  15.5 us (4%)
  between operations  13.5 us (4%)
  other arithmetic  11.4 us (3%)
    reduce_scatter x1, waiting for transfers between devices, local(): return lax.psum_scatter(partial_lags, 'tm', scatter_dimension=0, tiled=True)  104 us
    all_to_all x1, waiting for transfers between devices, lax.all_to_all(jnp.stack(lax.axis_size('chan') * [point], 0), 'chan', 0, 0)  90.2 us
    all_to_all x1, starting transfers between devices, lax.all_to_all(jnp.stack(lax.axis_size('chan') * [point], 0), 'chan', 0, 0)  15.3 us
    dot_general x8, matrix products, cross_spectrum(): jnp.einsum('kif,kjf->ijf', own_im, other_im, preferred_element_type=jnp.f...  15.1 us
    dot_general x8, matrix products, one_slab(): jnp.dot(half_spectra.reshape(-1, half_spectra.shape[-1]), lag_matrix, pre...  13.8 us
    while x112, local copies, waits for them, and re-layouts  12.4 us
    dynamic_slice x16, local copies, waits for them, and re-layouts, loop_body(): lax.dynamic_slice_in_dim(incoming, slab_index * slab_cols, slab_cols, 1)  11.9 us
    dot_general x8, local copies, waits for them, and re-layouts, cross_spectrum(): jnp.einsum('kif,kjf->ijf', own_im, other_im, preferred_element_type=jnp.f...  7.24 us
  transfers between devices with their start and end apart: 2, of which 2 were waited for; matrix products, arithmetic and copies ran while one was open for 1% of the time, Pallas kernels for 0%

profile of v1, /device:TPU:1, one launch (start us, length us, event | category | flops | bytes accessed | tf_op | source)
XLA Modules:
  0.0 344.1 jit_solution(5840409792115888566)
XLA Ops:
  6.5 6.2 %sine_negate_fusion = (f32[768,512]{1,0:T(8,128)S(1)}, f32[768,512]{1,0:T(8,128)S(1)}) fusion(), kind=kLoop, calls=%fused_computation.27 | loop fusion | flops 5898240 | bytes 3145728 | tf_op jit(solution)/shard_map/neg | solution.py:20
  15.0 2.5 stack.2
  17.5 15.3 %all-to-all-start = ((bf16[128,2,8,1024]{3,2,1,0:T(8,128)(2,1)}), bf16[128,2,8,1024]{3,2,1,0:T(8,128)(2,1)}, u32[]{:S(2)}, u32[]{:S(2)}) async-start(bf16[128,2,8,1024]{3,2,1,0:T(8,128)(2,1)} %stack.2), calls=%async_computation | async-start | bytes 8388608 | tf_op jit(solution)/shard_map/all_to_all | solution.py:11
  33.5 2.3 multiply_convert_fusion.1
  36.6 90.2 %all-to-all-done = bf16[128,2,8,1024]{3,2,1,0:T(8,128)(2,1)} async-done(((bf16[128,2,8,1024]{3,2,1,0:T(8,128)(2,1)}), bf16[128,2,8,1024]{3,2,1,0:T(8,128)(2,1)}, u32[]{:S(2)}, u32[]{:S(2)}) %all-to-all-start) | async-done | bytes 4194336 | tf_op jit(solution)/shard_map/all_to_all | solution.py:11
  126.8 4.7 %copy.14 = bf16[128,2,8,1024]{3,2,0,1:T(8,128)(2,1)} copy(bf16[128,2,8,1024]{3,2,1,0:T(8,128)(2,1)} %all-to-all-done) | data formatting | bytes 8388608 | tf_op jit(solution)/shard_map/all_to_all | solution.py:11
  131.6 3.9 %broadcast_in_dim.8 = f32[8,1024,256]{2,1,0:T(8,128)} broadcast(f32[]{:T(128)} %constant.72.clone.1), dimensions={} | broadcast | bytes 8388612 | tf_op jit(solution)/shard_map/broadcast_in_dim | solution.py:103
  135.5 97.5 %while.13 = (s32[]{:T(128)}, f32[8,1024,256]{2,1,0:T(8,128)}, bf16[2,1024,1024]{2,1,0:T(8,128)(2,1)}, bf16[2,8,1024]{1,0,2:T(2,128)(2,1)S(1)}, bf16[1024,256]{1,...) while((s32[]{:T(128)}, f32[8,1024,256]{2,1,0:T(8,128)}, bf16[2,1024,1024]{2,1,0:T(8,128)(2,1)}, ...), condition=%wide.region_3.4_spmd, body=%wide.region_2.3_spmd.sunk | while | flops 548405248 | bytes 29491544 | solution.py:92
  140.9 1.9 fusion.101
  146.0 1.7 fusion.102
  153.0 1.9 fusion.101
  158.1 1.7 fusion.102
  165.2 1.9 fusion.101
  170.3 1.7 fusion.102
  177.4 1.9 fusion.101
  189.5 1.9 fusion.101
  194.6 1.7 fusion.102
  201.7 1.9 fusion.101
  206.8 1.7 fusion.102
  213.9 1.9 fusion.101
  219.0 1.7 fusion.102
  226.1 1.9 fusion.101
  231.2 1.7 fusion.102
  233.0 104.2 %reduce-scatter.2.cloned.1.call-done = f32[4,1024,256]{2,1,0:T(8,128)} async-done(((f32[8,1024,256]{2,1,0:T(8,128)}), f32[4,1024,256]{2,1,0:T(8,128)}) %reduce-scatter.2.cloned.1.call-update) | async-done | bytes 4194320 | tf_op jit(solution)/shard_map/reduce_scatter | solution.py:107
  (215 shorter events, 73.5 us)
Async XLA Ops:
  6.5 6.2 %copy-start.9 = (s32[8]{0:T(128)S(1)}, s32[8]{0:T(128)}, u32[]{:S(2)}) copy-start(s32[8]{0:T(128)} %param.7) | copy-start | bytes 100
  6.5 6.2 %copy-start.8 = (s32[4]{0:T(128)S(1)}, s32[4]{0:T(128)}, u32[]{:S(2)}) copy-start(s32[4]{0:T(128)} %param.6) | copy-start | bytes 52
  6.5 6.4 %copy-start.7 = (f32[2,8,768]{2,1,0:T(8,128)S(1)}, f32[2,8,768]{2,1,0:T(8,128)}, u32[]{:S(2)}) copy-start(f32[2,8,768]{2,1,0:T(8,128)} %param.5) | copy-start | bytes 147460
  17.5 109.3 %all-to-all-start = ((bf16[128,2,8,1024]{3,2,1,0:T(8,128)(2,1)}), bf16[128,2,8,1024]{3,2,1,0:T(8,128)(2,1)}, u32[]{:S(2)}, u32[]{:S(2)}) async-start(bf16[128,2,8,1024]{3,2,1,0:T(8,128)(2,1)} %stack.2), calls=%async_computation | async-start | bytes 8388608 | tf_op jit(solution)/shard_map/all_to_all | solution.py:11
  32.8 304.4 %reduce-scatter.2.cloned.1.call-start = ((), (), s32[]{:S(2)}) async-start(), calls=%async_computation.2 | async-start | bytes 12582912 | tf_op jit(solution)/shard_map/reduce_scatter | solution.py:107
  135.5 4.4 %copy-start = (bf16[2,8,1024]{1,0,2:T(2,128)(2,1)}, bf16[2,8,1024]{1,0,2:T(2,128)(2,1)S(1)}, u32[]{:S(2)}) copy-start(bf16[2,8,1024]{1,0,2:T(2,128)(2,1)S(1)} %get-tuple-element.175) | copy-start | bytes 98308 | tf_op jit(solution)/shard_map/while
  140.9 1.9 copy-start.4
  147.7 4.4 %copy-start = (bf16[2,8,1024]{1,0,2:T(2,128)(2,1)}, bf16[2,8,1024]{1,0,2:T(2,128)(2,1)S(1)}, u32[]{:S(2)}) copy-start(bf16[2,8,1024]{1,0,2:T(2,128)(2,1)S(1)} %get-tuple-element.175) | copy-start | bytes 98308 | tf_op jit(solution)/shard_map/while
  153.0 1.9 copy-start.4
  159.8 4.4 %copy-start = (bf16[2,8,1024]{1,0,2:T(2,128)(2,1)}, bf16[2,8,1024]{1,0,2:T(2,128)(2,1)S(1)}, u32[]{:S(2)}) copy-start(bf16[2,8,1024]{1,0,2:T(2,128)(2,1)S(1)} %get-tuple-element.175) | copy-start | bytes 98308 | tf_op jit(solution)/shard_map/while
  165.2 1.9 copy-start.4
  172.0 4.4 %copy-start = (bf16[2,8,1024]{1,0,2:T(2,128)(2,1)}, bf16[2,8,1024]{1,0,2:T(2,128)(2,1)S(1)}, u32[]{:S(2)}) copy-start(bf16[2,8,1024]{1,0,2:T(2,128)(2,1)S(1)} %get-tuple-element.175) | copy-start | bytes 98308 | tf_op jit(solution)/shard_map/while
  177.4 1.9 copy-start.4
  184.2 4.4 %copy-start = (bf16[2,8,1024]{1,0,2:T(2,128)(2,1)}, bf16[2,8,1024]{1,0,2:T(2,128)(2,1)S(1)}, u32[]{:S(2)}) copy-start(bf16[2,8,1024]{1,0,2:T(2,128)(2,1)S(1)} %get-tuple-element.175) | copy-start | bytes 98308 | tf_op jit(solution)/shard_map/while
  189.5 1.9 copy-start.4
  194.6 1.7 copy-start.1
  196.4 4.4 %copy-start = (bf16[2,8,1024]{1,0,2:T(2,128)(2,1)}, bf16[2,8,1024]{1,0,2:T(2,128)(2,1)S(1)}, u32[]{:S(2)}) copy-start(bf16[2,8,1024]{1,0,2:T(2,128)(2,1)S(1)} %get-tuple-element.175) | copy-start | bytes 98308 | tf_op jit(solution)/shard_map/while
  201.7 1.9 copy-start.4
  206.8 1.7 copy-start.1
  208.6 4.4 %copy-start = (bf16[2,8,1024]{1,0,2:T(2,128)(2,1)}, bf16[2,8,1024]{1,0,2:T(2,128)(2,1)S(1)}, u32[]{:S(2)}) copy-start(bf16[2,8,1024]{1,0,2:T(2,128)(2,1)S(1)} %get-tuple-element.175) | copy-start | bytes 98308 | tf_op jit(solution)/shard_map/while
  213.9 1.9 copy-start.4
  219.0 1.7 copy-start.1
  220.8 4.4 %copy-start = (bf16[2,8,1024]{1,0,2:T(2,128)(2,1)}, bf16[2,8,1024]{1,0,2:T(2,128)(2,1)S(1)}, u32[]{:S(2)}) copy-start(bf16[2,8,1024]{1,0,2:T(2,128)(2,1)S(1)} %get-tuple-element.175) | copy-start | bytes 98308 | tf_op jit(solution)/shard_map/while
  226.1 1.9 copy-start.4
  (37 other events, 41.9 us)
Sparse Core Ops, SparseCore 0:
  233.1 104.0 reduce-scatter.1
